TPU v7x, 32 devices: a whole 2x2x4 slice. The times are simulated.
32 devices in a mesh: fold: 4 (over y, x), trow: 4 (over z), tcol: 2 (over core).
Axes of the slice: x: 2, y: 2, z: 4, core: 2. Of those that a mesh axis runs over, the one named last changes fastest.
Arguments:
- samples: bfloat16 [8, 2048, 256], P('fold', ('trow', 'tcol')), may hold values from -6 to 6
- targets: bfloat16 [8, 2048, 128], P('fold', ('trow', 'tcol')), may hold values from -6 to 6
- frequencies: bfloat16 [256, 4096], replicated, may hold values from -1.5 to 1.5
- phases: float32 [4096], replicated, may hold values from -3.140625 to 3.140625
- valid_rows: int32 [8], P('fold'), may hold values from 1024 to 2048
- ridge: float32 [8], P('fold'), may hold values from 0.1 to 1
- low_bound: float32 [8], P('fold'), may hold values from 0.05 to 0.4
- high_bound: float32 [8], P('fold'), may hold values from 9 to 12
Outputs:
- iterate: float32 [8, 4096, 128], P('fold', 'tcol')
- residual: float32 [8, 4096, 128], P('fold', 'tcol')
Inputs may be any that keep to these rules, and one draw needn't show every extreme that they name: Rows of fold k at positions valid_rows[k] and beyond take no part in any fit.
All inputs are finite; a program needn't handle non-finite values.
Results may differ from a plain program's by a relative error of at most 0.0046.
Values may be sent and summed in bfloat16 or wider, within the bound.
A program may use at most 128 MiB of HBM per device.

v0:
```python
import math

import jax
import jax.numpy as jnp
from jax import lax
from jax.sharding import PartitionSpec as P

ITERS = 2


root_two = math.sqrt(2.0)


def entering(part, axis, combine, identity):
    place = lax.axis_index(axis)
    gathered = jax.tree.map(lambda a: lax.all_gather(a, axis), part)
    state = jax.tree.map(lambda a, e: jnp.zeros_like(a) + jnp.asarray(e, a.dtype), part, identity)

    def one(hop, state):
        return combine(
            state, jax.tree.map(lambda a: lax.dynamic_index_in_dim(a, hop, 0, False), gathered)
        )

    return lax.fori_loop(0, place, one, state)


def cosine_block(sample_rows, freq_cols, phase_cols, valid):
    angles = (
        jnp.einsum("fkr,rc->fkc", sample_rows, freq_cols, preferred_element_type=jnp.float32)
        + phase_cols
    )
    positions = lax.iota(jnp.int32, sample_rows.shape[1])
    keep = (positions[None, :] < valid[:, None]).astype(jnp.float32)
    return (root_two * jnp.cos(angles) * keep[:, :, None]).astype(jnp.bfloat16)


def accumulate(left_feat, right_feat, target_rows):
    gram_sum = jnp.einsum("fka,fkb->fab", left_feat, right_feat, preferred_element_type=jnp.float32)
    cross_sum = jnp.einsum(
        "fkb,fkt->fbt", right_feat, target_rows, preferred_element_type=jnp.float32
    )
    return (gram_sum, cross_sum)


def combine_sums(earlier, later):
    return tuple((former + latter for former, latter in zip(earlier, later)))


def apply_tile(matrix, direction, row_start, row_count):
    block = direction.shape[1]
    offset = row_start % block
    mine = lax.dynamic_slice_in_dim(direction, offset, row_count, 1)
    pieces = lax.all_gather(mine, "tcol", axis=1, tiled=True)
    owner = row_start // block
    needed = lax.dynamic_slice_in_dim(pieces, owner * row_count, row_count, 1)
    return jnp.einsum("fab,fat->fbt", matrix, needed, precision=lax.Precision.HIGHEST)


def on_device(samples, targets, frequencies, phases, valid_rows, ridge, low_bound, high_bound):
    width = frequencies.shape[1]
    left_width = width // lax.axis_size("trow")
    right_width = width // lax.axis_size("tcol")
    left_start = lax.axis_index("trow") * left_width
    right_start = lax.axis_index("tcol") * right_width
    left_freq = lax.dynamic_slice_in_dim(frequencies, left_start, left_width, 1)
    right_freq = lax.dynamic_slice_in_dim(frequencies, right_start, right_width, 1)
    left_phase = lax.dynamic_slice_in_dim(phases, left_start, left_width, 0)
    right_phase = lax.dynamic_slice_in_dim(phases, right_start, right_width, 0)
    pieces = (
        lax.all_gather(samples, ("trow", "tcol"), axis=1, tiled=True),
        lax.all_gather(targets, ("trow", "tcol"), axis=1, tiled=True),
    )
    left_feat = cosine_block(pieces[0], left_freq, left_phase, valid_rows)
    right_feat = cosine_block(pieces[0], right_freq, right_phase, valid_rows)
    gram_sum, cross_sum = accumulate(left_feat, right_feat, pieces[1])
    counts = jnp.cumsum(valid_rows.astype(jnp.float32))
    gram_run = jnp.cumsum(gram_sum, axis=0)
    cross_run = jnp.cumsum(cross_sum, axis=0)
    identity = (
        jnp.zeros_like(gram_run[0]),
        jnp.zeros_like(cross_run[0]),
        jnp.zeros((), jnp.float32),
    )
    earlier = entering((gram_run[-1], cross_run[-1], counts[-1]), "fold", combine_sums, identity)
    prefix_count = counts + earlier[2]
    matrix = (gram_run + earlier[0][None]) / prefix_count[:, None, None]
    right_side = (cross_run + earlier[1][None]) / jnp.sqrt(prefix_count)[:, None, None]
    center = ((high_bound + low_bound) / 2.0 + ridge)[:, None, None]
    spread = ((high_bound - low_bound) / 2.0)[:, None, None]
    shift = ridge[:, None, None]
    sigma = center / spread
    rho = 1.0 / sigma
    iterate = jnp.zeros_like(right_side)
    direction = right_side / center
    residual = right_side
    for iteration in range(ITERS):
        iterate = iterate + direction
        partial_image = apply_tile(matrix, direction, left_start, left_width)
        image = lax.psum(partial_image, "trow") + shift * direction
        residual = residual - image
        if iteration + 1 < ITERS:
            rho_next = 1.0 / (2.0 * sigma - rho)
            direction = rho_next * rho * direction + 2.0 * rho_next / spread * residual
            rho = rho_next
    return (iterate, residual)


def solution(mesh):
    in_specs = (
        P("fold", ("trow", "tcol"), None),
        P("fold", ("trow", "tcol"), None),
        P(),
        P(),
        P("fold"),
        P("fold"),
        P("fold"),
        P("fold"),
    )
    out_specs = (P("fold", "tcol", None), P("fold", "tcol", None))
    return jax.shard_map(
        on_device, mesh=mesh, in_specs=in_specs, out_specs=out_specs, check_vma=False
    )
```

profile of v0, /device:TPU:0, one launch (start us, length us, event | category | flops | bytes accessed | tf_op | source)
XLA Modules:
  0.0 894.5 jit_solution(9763020037538166782)
XLA Ops:
  10.2 31.3 %all-gather.8.cloned.1.call-done = bf16[2,2048,256]{2,1,0:T(8,128)(2,1)} async-done(((bf16[2,256,256]{2,1,0:T(8,128)(2,1)}), bf16[2,2048,256]{2,1,0:T(8,128)(2,1)}) %all-gather.8.cloned.1.call-update) | async-done | bytes 2097168 | tf_op jit(solution)/shard_map/all_gather | solution.py:70
  41.5 116.6 %fusion = bf16[2,2048,2048]{1,2,0:T(8,128)(2,1)} fusion(f32[2,2048]{1,0:T(2,128)S(1)} %compare_select_fusion, f32[2048]{0:T(1024)S(1)} %dynamic_slice.37, bf16[2,2048,256]{2,1,0:T(8,128)(2,1)} %all-gather.8.cloned.1.call-done, bf16[256,4096]{1,0:T(8,128)(2,1)S(1)} %copy-done, s32[]{:T(128)S(6)} %select_n.38), kind=kOutput, calls=%fused_computation.3 | convolution fusion | flops 4320133120 | bytes 19947524 | tf_op jit(solution)/shard_map/fkr,rc->fkc/dot_general | solution.py:29
  158.0 8.4 fusion.29
  166.8 1.3 copy-done.2
  168.1 1.0 slice.17
  169.4 58.4 %fusion.51 = bf16[2,2048,1024]{1,2,0:T(8,128)(2,1)S(1)} fusion(f32[2,2048]{1,0:T(2,128)S(1)} %compare_select_fusion, f32[1024]{0:T(1024)S(1)} %dynamic-slice-done, bf16[2,2048,256]{2,1,0:T(8,128)(2,1)} %all-gather.8.cloned.1.call-done, bf16[256,4096]{1,0:T(8,128)(2,1)S(1)} %copy-done, s32[]{:T(128)} %select_n.39), kind=kOutput, calls=%fused_computation.6.clone.clone.1 | convolution fusion | flops 2160066560 | bytes 11030532 | tf_op jit(solution)/shard_map/fkr,rc->fkc/dot_general | solution.py:29
  227.8 22.4 %fusion.2 = f32[2,1024,2048]{2,1,0:T(8,128)} fusion(bf16[2,2048,2048]{1,2,0:T(8,128)(2,1)} %fusion, bf16[2,2048,1024]{1,2,0:T(8,128)(2,1)S(1)} %fusion.51), kind=kOutput, calls=%fused_computation.7 | convolution fusion | flops 17179869184 | bytes 41943040 | tf_op jit(solution)/shard_map/fka,fkb->fab/dot_general | solution.py:38
  250.1 11.8 %fusion.28 = f32[2,1024,2048]{2,1,0:T(8,128)} fusion(f32[2,1024,2048]{2,1,0:T(8,128)} %fusion.2), kind=kOutput, calls=%fused_computation.43 | output fusion | flops 4194304 | bytes 33554432 | tf_op jit(solution)/shard_map/jit(cumsum)/reduce_window_sum | solution.py:77
  262.0 7.7 slice.16
  271.8 1.2 bitcast_dynamic-update-slice_fusion
  273.0 9.9 %all-reduce = f32[4]{0:T(128)S(1)} all-reduce(f32[4]{0:T(128)S(1)} %bitcast_dynamic-update-slice_fusion), channel_id=2, replica_groups=mesh['fold'=4,'trow'=4,'tcol'=2] {'fold'}, use_global_device_ids=true, to_apply=%add | all-reduce | flops 4 | bytes 32 | tf_op jit(solution)/shard_map/all_gather | solution.py:16
  282.9 283.8 %all-gather.12.cloned.1.call-done = f32[4,1024,2048]{2,1,0:T(8,128)} async-done(((f32[1,1024,2048]{2,1,0:T(8,128)}), f32[4,1024,2048]{2,1,0:T(8,128)}) %all-gather.12.cloned.1.call-update) | async-done | bytes 33554448 | tf_op jit(solution)/shard_map/all_gather | solution.py:16
  566.7 4.3 broadcast_in_dim.4
  573.0 1.0 constant_dynamic-slice_fusion.1
  574.1 14.4 %add_divide_fusion = f32[2,1024,2048]{2,1,0:T(8,128)} fusion(f32[2,1024,2048]{2,1,0:T(8,128)} %fusion.28, f32[2]{0:T(128)S(1)} %get-tuple-element.69, f32[1024,2048]{1,0:T(8,128)} %get-tuple-element.49), kind=kLoop, calls=%fused_computation.4 | loop fusion | flops 8388608 | bytes 41943048 | tf_op jit(solution)/shard_map/div | solution.py:86
  588.5 38.0 %all-gather.16.cloned.1.call-done = f32[2,2048,128]{2,1,0:T(8,128)} async-done(((f32[2,1024,128]{2,1,0:T(8,128)}), f32[2,2048,128]{2,1,0:T(8,128)}) %all-gather.16.cloned.1.call-update) | async-done | bytes 2097168 | tf_op jit(solution)/shard_map/all_gather | solution.py:53
  626.5 30.2 %fusion.11 = f32[2,2048,128]{2,1,0:T(8,128)} fusion(f32[2,1024,2048]{2,1,0:T(8,128)} %add_divide_fusion, f32[2,2048,128]{2,1,0:T(8,128)} %all-gather.16.cloned.1.call-done, s32[]{:T(128)S(6)} %select_n.43), kind=kOutput, calls=%fused_computation.18 | convolution fusion | flops 6442450944 | bytes 19922948 | tf_op jit(solution)/shard_map/fab,fat->fbt/dot_general | solution.py:56
  657.1 90.8 %all-reduce.4.cloned.1.call-done = f32[2,2048,128]{2,1,0:T(8,128)} async-done(((f32[2,2048,128]{2,1,0:T(8,128)}), f32[2,2048,128]{2,1,0:T(8,128)}) %all-reduce.4.cloned.1.call-update) | async-done | bytes 2097168 | tf_op jit(solution)/shard_map/psum | solution.py:99
  747.9 3.7 fusion.24
  751.5 1.3 copy-done.4
  753.9 9.6 %all-gather.18.cloned.1.call-done = f32[2,2048,128]{2,1,0:T(8,128)} async-done(((f32[2,1024,128]{2,1,0:T(8,128)}), f32[2,2048,128]{2,1,0:T(8,128)}) %all-gather.18.cloned.1.call-update) | async-done | bytes 2097168 | tf_op jit(solution)/shard_map/all_gather | solution.py:53
  763.6 30.2 %fusion.9 = f32[2,2048,128]{2,1,0:T(8,128)} fusion(f32[2,1024,2048]{2,1,0:T(8,128)} %add_divide_fusion, f32[2,2048,128]{2,1,0:T(8,128)} %all-gather.18.cloned.1.call-done, s32[]{:T(128)S(6)} %select_n.43), kind=kOutput, calls=%fused_computation.16 | convolution fusion | flops 6442450944 | bytes 19922948 | tf_op jit(solution)/shard_map/fab,fat->fbt/dot_general | solution.py:56
  793.8 87.8 %all-reduce.6.cloned.1.call-done = f32[2,2048,128]{2,1,0:T(8,128)} async-done(((f32[2,2048,128]{2,1,0:T(8,128)}), f32[2,2048,128]{2,1,0:T(8,128)}) %all-reduce.6.cloned.1.call-update) | async-done | bytes 2097168 | tf_op jit(solution)/shard_map/psum | solution.py:99
  881.6 5.6 add_subtract_fusion
  (54 shorter events, 9.0 us)
Async XLA Ops:
  7.2 34.3 %copy-start = (bf16[256,4096]{1,0:T(8,128)(2,1)S(1)}, bf16[256,4096]{1,0:T(8,128)(2,1)}, u32[]{:S(2)}) copy-start(bf16[256,4096]{1,0:T(8,128)(2,1)} %param.12) | copy-start | bytes 6291460
  7.2 34.3 %all-gather.8.cloned.1.call-start = ((), (), s32[]{:S(2)}) async-start(), calls=%async_computation | async-start | bytes 2359296 | tf_op jit(solution)/shard_map/all_gather | solution.py:70
  7.9 150.1 %all-gather.10.cloned.1.call-start = ((), (), s32[]{:S(2)}) async-start(), calls=%async_computation.1 | async-start | bytes 1179648 | tf_op jit(solution)/shard_map/all_gather | solution.py:71
  8.7 274.2 %all-gather.14.cloned.1.call-start = ((), (), s32[]{:S(2)}) async-start(), calls=%async_computation.3 | async-start | bytes 5242880 | tf_op jit(solution)/shard_map/all_gather | solution.py:16
  166.8 1.3 copy-start.2
  168.1 1.3 dynamic-slice-start
  169.1 397.5 %all-gather.12.cloned.1.call-start = ((), (), s32[]{:S(2)}) async-start(), calls=%async_computation.2 | async-start | bytes 41943040 | tf_op jit(solution)/shard_map/all_gather | solution.py:16
  269.7 0.7 copy-start.8
  269.7 1.4 copy-start.9
  269.8 356.8 %all-gather.16.cloned.1.call-start = ((), (), s32[]{:S(2)}) async-start(), calls=%async_computation.4 | async-start | bytes 3145728 | tf_op jit(solution)/shard_map/all_gather | solution.py:53
  571.0 0.7 copy-start.5
  571.0 0.7 copy-start.6
  571.0 0.7 copy-start.7
  571.0 1.6 copy-start.3
  574.0 173.8 %all-reduce.4.cloned.1.call-start = ((), (), s32[]{:S(2)}) async-start(), calls=%async_computation.5 | async-start | bytes 4194304 | tf_op jit(solution)/shard_map/psum | solution.py:99
  656.8 106.8 %all-gather.18.cloned.1.call-start = ((), (), s32[]{:S(2)}) async-start(), calls=%async_computation.6 | async-start | bytes 3145728 | tf_op jit(solution)/shard_map/all_gather | solution.py:53
  751.5 1.3 copy-start.4
  753.9 127.8 %all-reduce.6.cloned.1.call-start = ((), (), s32[]{:S(2)}) async-start(), calls=%async_computation.7 | async-start | bytes 4194304 | tf_op jit(solution)/shard_map/psum | solution.py:99
  881.6 5.6 copy-start.1
Sparse Core Ops, SparseCore 0:
  9.6 31.7 all-gather.7
  43.1 21.6 all-gather.9
  169.3 52.1 all-gather.13
  269.9 296.6 all-gather.11
  574.1 52.3 all-gather.15
  656.9 90.9 all-reduce.3
  754.0 9.5 all-gather.17
  793.9 87.6 all-reduce.5
where the time goes:
time: 902 us; the launch traced here: 895 us
  waiting for transfers between devices  543 us (60%)
  matrix products  266 us (29%)
  other arithmetic  37.1 us (4%)
  local copies, waits for them, and re-layouts  23.1 us (3%)
  between operations  14.7 us (2%)
  blocking collectives  9.85 us (1%)
    all_gather x2, waiting for transfers between devices, entering(): gathered = jax.tree.map(lambda a: lax.all_gather(a, axis), part)  284 us
    psum x2, waiting for transfers between devices, on_device(): image = lax.psum(partial_image, 'trow') + shift * direction  179 us
    dot_general x2, matrix products, cosine_block(): jnp.einsum('fkr,rc->fkc', sample_rows, freq_cols, preferred_element_type=...  175 us
    dot_general x2, matrix products, apply_tile(): jnp.einsum('fab,fat->fbt', matrix, needed, precision=lax.Precision.HIGHEST)  60.4 us
    all_gather x2, waiting for transfers between devices, apply_tile(): pieces = lax.all_gather(mine, 'tcol', axis=1, tiled=True)  47.7 us
    all_gather x1, waiting for transfers between devices, on_device(): lax.all_gather(samples, ('trow', 'tcol'), axis=1, tiled=True)  31.3 us
    dot_general x1, matrix products, accumulate(): jnp.einsum('fka,fkb->fab', left_feat, right_feat, preferred_element_type=...  22.4 us
  transfers between devices with their start and end apart: 8, of which 6 were waited for; matrix products, arithmetic and copies ran while one was open for 26% of the time, Pallas kernels for 0%

commit v1 on v0

v1 whole, which is shorter than its diff:
```python
import math

import jax
import jax.numpy as jnp
import numpy as np
from jax import lax
from jax.sharding import PartitionSpec as P

ITERS = 2
SINE = (3.141582022142075, -5.16714279609351, 2.5418990253836506, -0.5546361920474749)


def pair_table(chips, cores):
    per = chips // (2 * cores)
    table = np.zeros((chips, cores, 2, per), np.int32)
    for z in range(chips):
        if z == 0:
            pairs = [(2 * per * c + i, 2 * per * c + per + i) for c in range(cores) for i in range(per)]
        else:
            pairs = [(a, a ^ z) for a in range(chips) if a < a ^ z]
        table[z] = np.array(pairs, np.int32).reshape(cores, per, 2).transpose(0, 2, 1)
    return table


def features(sample_rows, freq_cols, phase_cols, valid):
    angles = jnp.einsum("fkr,rc->fkc", sample_rows, freq_cols, preferred_element_type=jnp.float32)
    turn = np.float32(0.5 / math.pi)
    turns = angles * turn + phase_cols * turn
    rest = turns - jnp.round(turns)
    square = rest * rest
    poly = np.float32(SINE[3])
    for coef in SINE[2::-1]:
        poly = poly * square + np.float32(coef)
    sine = poly * rest * np.float32(2.0 ** 0.75)
    positions = lax.iota(jnp.int32, sample_rows.shape[1])
    keep = positions[None, :] < valid[:, None]
    return jnp.where(keep[:, :, None], np.float32(math.sqrt(2.0)) - sine * sine, 0.0).astype(jnp.bfloat16)


def fold_prefix(total, wire):
    size = lax.axis_size("fold")
    place = lax.axis_index("fold")
    earlier = jnp.zeros_like(total)
    step = 1
    while step < size:
        last = 2 * step >= size
        pairs = [(i, i ^ step) for i in range(size) if not (last and i & step)]
        got = lax.ppermute(total.astype(wire), "fold", pairs).astype(total.dtype)
        earlier = earlier + jnp.where((place & step) != 0, got, 0)
        total = total + got
        step *= 2
    return earlier


def halves(x):
    high = x.astype(jnp.bfloat16)
    return high, (x - high.astype(jnp.float32)).astype(jnp.bfloat16)


def product(spec, a, b):
    dot = lambda x, y: jnp.einsum(spec, x, y, preferred_element_type=jnp.float32)
    return dot(a[0], b[0]) + dot(a[0], b[1]) + dot(a[1], b[0])


def on_device(samples, targets, frequencies, phases, valid_rows, ridge, low_bound, high_bound):
    width = frequencies.shape[1]
    chips, cores = lax.axis_size("trow"), lax.axis_size("tcol")
    z, c = lax.axis_index("trow"), lax.axis_index("tcol")
    w = width // chips
    table = pair_table(chips, cores)
    per = table.shape[3]
    tgt = targets.shape[2]
    nf = samples.shape[0]
    ids = jnp.asarray(table)[z, c].reshape(2 * per)
    freq_cols = jnp.take(frequencies.reshape(-1, chips, w), ids, axis=1).reshape(-1, 2 * per * w)
    phase_cols = jnp.take(phases.reshape(chips, w), ids, axis=0).reshape(-1)
    rows = lax.all_gather(samples, ("trow", "tcol"), axis=1, tiled=True)
    target_rows = lax.all_gather(targets, ("trow", "tcol"), axis=1, tiled=True)
    feat = features(rows, freq_cols, phase_cols, valid_rows)
    feat = feat.reshape(nf, feat.shape[1], 2, per, w)
    left, right = feat[:, :, 0], feat[:, :, 1]
    counts = jnp.cumsum(valid_rows.astype(jnp.float32))

    part = w // chips
    mine = lax.dynamic_slice_in_dim(feat, z * part, part, 4)
    cross = jnp.einsum("fksaw,fkt->fsawt", mine, target_rows, preferred_element_type=jnp.float32)
    cross = jnp.cumsum(cross.reshape(nf, 2 * per, part, tgt), axis=0)
    cross = cross + fold_prefix(cross[-1], jnp.float32)[None]
    prefix_count = counts + fold_prefix(counts[-1:], jnp.float32)
    cross = cross / jnp.sqrt(prefix_count)[:, None, None, None]
    everyone = lax.all_gather(cross, ("trow", "tcol"), axis=0)
    everyone = jnp.moveaxis(everyone, 2, 1).reshape(-1, nf, part, tgt)
    source = np.zeros((chips, chips), np.int32)
    for k, block in enumerate(table.reshape(-1)):
        source[block, k // (cores * 2 * per)] = k
    right_side = jnp.take(everyone, source.reshape(-1), axis=0)
    right_side = jnp.moveaxis(right_side, 1, 0).reshape(nf, chips, w, tgt)

    diagonal = z == 0
    first = jnp.where(diagonal, left, right)
    second = jnp.where(diagonal, right, left)
    upper = lax.broadcasted_iota(jnp.int32, (w, w), 0) <= lax.broadcasted_iota(jnp.int32, (w, w), 1)
    same = jnp.eye(w, dtype=bool)
    gram_one = jnp.einsum("fkma,fkmb->fmab", left, first, preferred_element_type=jnp.float32)
    gram_two = jnp.einsum("fkma,fkmb->fmab", second, right, preferred_element_type=jnp.float32)
    half = jnp.where(jnp.logical_and(diagonal, same), 0.5, 1.0).astype(jnp.float32)
    tile = jnp.where(upper, gram_one, gram_two) * half
    own = jnp.where(diagonal, jnp.sum(right.astype(jnp.float32) ** 2, axis=1), 0.0)
    tile = jnp.cumsum(tile, axis=0)
    own = jnp.cumsum(own, axis=0)
    tile = (tile + fold_prefix(tile[-1], jnp.bfloat16)[None]) / prefix_count[:, None, None, None]
    own = (own + fold_prefix(own[-1], jnp.float32)[None]) / prefix_count[:, None, None]
    high, low = halves(tile)
    zero = jnp.zeros((), jnp.bfloat16)
    above = (jnp.where(upper, high, zero), jnp.where(upper, low, zero))
    below = (jnp.where(upper, zero, high), jnp.where(upper, zero, low))

    def apply(direction):
        mine = jnp.take(direction, ids, axis=1).reshape(nf, 2, per, w, tgt)
        dl, dr = mine[:, 0], mine[:, 1]
        hl, hr = halves(dl), halves(dr)
        pick = lambda a, b: tuple(jnp.where(diagonal, i, j) for i, j in zip(a, b))
        one = product("fmab,fmbt->fmat", above, pick(hl, hr))
        two = product("fmab,fmbt->fmat", below, hr)
        three = product("fmab,fmat->fmbt", above, hl)
        four = product("fmab,fmat->fmbt", below, pick(hr, hl))
        out_l = one + jnp.where(diagonal, three, two)
        out_r = four + jnp.where(diagonal, two, three) + own[..., None] * dr
        both = jnp.stack((out_l, out_r), 1).reshape(nf, 2 * per, w, tgt)
        both = lax.all_gather(both, "tcol", axis=1, tiled=True)
        chip_ids = jnp.asarray(table)[z].reshape(-1)
        order = jnp.argsort(chip_ids)
        wanted = lax.dynamic_slice_in_dim(order, c * (chips // cores), chips // cores, 0)
        return lax.psum(jnp.take(both, wanted, axis=1), "trow")

    expand = lambda x: x[:, None, None, None]
    share = chips // cores
    right_side_mine = lax.dynamic_slice_in_dim(right_side, c * share, share, 1)
    center = expand((high_bound + low_bound) / 2.0 + ridge)
    spread = expand((high_bound - low_bound) / 2.0)
    shift = expand(ridge)
    sigma = center / spread
    rho = 1.0 / sigma
    whole = right_side / center
    direction = right_side_mine / center
    iterate = jnp.zeros_like(direction)
    residual = right_side_mine
    for iteration in range(ITERS):
        iterate = iterate + direction
        residual = residual - (apply(whole) + shift * direction)
        if iteration + 1 < ITERS:
            rho_next = 1.0 / (2.0 * sigma - rho)
            direction = rho_next * rho * direction + 2.0 * rho_next / spread * residual
            rho = rho_next
            whole = lax.all_gather(direction, "tcol", axis=1, tiled=True)
    shape = (nf, share * w, tgt)
    return (iterate.reshape(shape), residual.reshape(shape))


def solution(mesh):
    in_specs = (
        P("fold", ("trow", "tcol"), None),
        P("fold", ("trow", "tcol"), None),
        P(),
        P(),
        P("fold"),
        P("fold"),
        P("fold"),
        P("fold"),
    )
    out_specs = (P("fold", "tcol", None), P("fold", "tcol", None))
    return jax.shard_map(
        on_device, mesh=mesh, in_specs=in_specs, out_specs=out_specs, check_vma=False
    )
```

time: 902 us -> 565 us (0.63)
  waiting for transfers between devices: 543 us -> 296 us
  matrix products: 266 us -> 98.5 us
  local copies, waits for them, and re-layouts: 23.1 us -> 66 us
  other arithmetic: 37.1 us -> 65.6 us
  starting transfers between devices: 0.75 us -> 18.8 us
  blocking collectives: 9.85 us -> 0 us
    all_gather x6, waiting for transfers between devices: 363 us -> 40.5 us  [the longest x2 26.7 us: apply(): both = lax.all_gather(both, 'tcol', axis=1, tiled=True)]
    dot_general x6 -> x28, matrix products: 266 us -> 98.5 us  [the longest x24 36.8 us: product(): jnp.einsum(spec, x, y, preferred_element_type=jnp.float32)]
    ppermute x0 -> x8, waiting for transfers between devices: none -> 81.9 us  [fold_prefix(): got = lax.ppermute(total.astype(wire), 'fold', pairs).astype(total.dtype)]
    gather x0 -> x8, local copies, waits for them, and re-layouts: none -> 25.6 us  [the longest x2 8.37 us: apply(): mine = jnp.take(direction, ids, axis=1).reshape(nf, 2, per, w, tgt)]
    ppermute x0 -> x8, starting transfers between devices: none -> 18.2 us  [fold_prefix(): got = lax.ppermute(total.astype(wire), 'fold', pairs).astype(total.dtype)]
    select_n x0 -> x7, other arithmetic: none -> 13.7 us  [the longest x2 4.62 us: apply(): return lax.psum(jnp.take(both, wanted, axis=1), 'trow')]
    all_gather x0 -> x3, local copies, waits for them, and re-layouts: none -> 13.7 us  [the longest x2 9 us: apply(): both = lax.all_gather(both, 'tcol', axis=1, tiled=True)]
    div x2 -> x4, other arithmetic: 14.7 us -> 3.28 us  [the longest x1 2.29 us: on_device(): whole = right_side / center]
  transfers between devices with their start and end apart: 8 -> 16, of which waited for: 6 -> 10; matrix products, arithmetic and copies ran while one was open for 26% -> 22% of each run, Pallas kernels for 0% -> 0%
where the time goes in v1:
time: 565 us; the launch traced here: 562 us
  waiting for transfers between devices  296 us (52%)
  matrix products  98.5 us (17%)
  local copies, waits for them, and re-layouts  66 us (12%)
  other arithmetic  65.6 us (12%)
  starting transfers between devices  18.8 us (3%)
  between operations  17.5 us (3%)
    psum x2, waiting for transfers between devices, apply(): return lax.psum(jnp.take(both, wanted, axis=1), 'trow')  172 us
    ppermute x8, waiting for transfers between devices, fold_prefix(): got = lax.ppermute(total.astype(wire), 'fold', pairs).astype(total.dtype)  81.9 us
    dot_general x24, matrix products, product(): jnp.einsum(spec, x, y, preferred_element_type=jnp.float32)  36.8 us
    all_gather x2, waiting for transfers between devices, apply(): both = lax.all_gather(both, 'tcol', axis=1, tiled=True)  26.7 us
    dot_general x1, matrix products, features(): jnp.einsum('fkr,rc->fkc', sample_rows, freq_cols, preferred_element_type=...  24 us
    ppermute x8, starting transfers between devices, fold_prefix(): got = lax.ppermute(total.astype(wire), 'fold', pairs).astype(total.dtype)  18.2 us
    dot_general x1, matrix products, on_device(): jnp.einsum('fkma,fkmb->fmab', second, right, preferred_element_type=jnp.f...  17 us
    dot_general x1, matrix products, on_device(): jnp.einsum('fkma,fkmb->fmab', left, first, preferred_element_type=jnp.flo...  16.9 us
  transfers between devices with their start and end apart: 16, of which 10 were waited for; matrix products, arithmetic and copies ran while one was open for 22% of the time, Pallas kernels for 0%

profile of v1, /device:TPU:0, one launch (start us, length us, event | category | flops | bytes accessed | tf_op | source)
XLA Modules:
  0.0 562.0 jit_solution(15391721637189208998)
XLA Ops:
  34.3 4.6 collective-permute-start.3
  41.4 24.0 %select_convert_fusion = bf16[2,2048,2048]{1,2,0:T(8,128)(2,1)} fusion(f32[2048]{0:T(1024)S(1)} %fusion.57, pred[2,2048]{1,0:T(4,128)(4,1)S(1)} %iota_compare_fusion.2, bf16[2,2048,256]{2,1,0:T(8,128)(2,1)} %all-gather.9.cloned.1.call-done, bf16[256,2048]{0,1:T(8,128)(2,1)S(1)} %copy-done.9), kind=kOutput, calls=%fused_computation.8 | convolution fusion | flops 4437573632 | bytes 19935232 | tf_op jit(solution)/shard_map/fkr,rc->fkc/dot_general | solution.py:26
  65.4 16.9 %fusion.3 = f32[2,1024,1024]{2,1,0:T(8,128)} fusion(pred[]{:T(512)S(6)} %eq.10, bf16[2,2048,2,1,1024]{1,4,2,0,3:T(8,128)(2,1)} %bitcast.213), kind=kOutput, calls=%fused_computation.14 | convolution fusion | flops 8594128896 | bytes 33554432 | tf_op jit(solution)/shard_map/fkma,fkmb->fmab/dot_general | solution.py:104
  82.3 17.0 %fusion.1 = f32[2,1024,1024]{2,1,0:T(8,128)} fusion(pred[]{:T(512)S(6)} %eq.10, bf16[2,2048,2,1,1024]{1,4,2,0,3:T(8,128)(2,1)} %bitcast.214), kind=kOutput, calls=%fused_computation.12 | convolution fusion | flops 8594128896 | bytes 33554432 | tf_op jit(solution)/shard_map/fkma,fkmb->fmab/dot_general | solution.py:105
  104.9 10.1 %fusion.8 = f32[2,1,1024,1024]{3,2,0,1:T(8,128)} fusion(f32[2,1024,1024]{2,1,0:T(8,128)} %fusion.3, f32[2,1024,1024]{2,1,0:T(8,128)} %fusion.1, f32[1024,1024]{1,0:T(8,128)S(1)} %copy-done.6, pred[1024,1024]{1,0:T(8,128)(4,1)S(1)} %iota_compare_fusion.1), kind=kOutput, calls=%fused_computation.21 | output fusion | flops 6291456 | bytes 30408704 | tf_op jit(solution)/shard_map/jit(cumsum)/reduce_window_sum | solution.py:109
  125.5 44.7 %collective-permute-done.4 = bf16[1,1024,1024]{2,1,0:T(8,128)(2,1)} collective-permute-done((bf16[1,1024,1024]{2,1,0:T(8,128)(2,1)}, bf16[1,1024,1024]{2,1,0:T(8,128)(2,1)}, u32[]{:S(2)}, u32[]{:S(2)}) %collective-permute-start.4) | collective-permute-done | bytes 2097184 | tf_op jit(solution)/shard_map/ppermute | solution.py:48
  170.2 4.9 fusion.18
  178.0 5.1 multiply_reduce_fusion
  188.2 33.0 %collective-permute-done.7 = f32[1,1024]{1,0:T(1,128)S(1)} collective-permute-done((f32[1,1024]{1,0:T(1,128)S(1)}, f32[1,1024]{1,0:T(1,128)S(1)}, u32[]{:S(2)}, u32[]{:S(2)}) %collective-permute-start.7) | collective-permute-done | bytes 4128 | tf_op jit(solution)/shard_map/ppermute | solution.py:48
  224.6 5.9 %subtract_convert_fusion = bf16[2,1024,1024]{2,1,0:T(8,128)(2,1)} fusion(f32[2]{0:T(128)S(1)} %get-tuple-element.18, f32[1024,1024]{1,0:T(8,128)S(1)} %fusion.17, f32[2,1,1024,1024]{3,2,0,1:T(8,128)} %fusion.8), kind=kLoop, calls=%fused_computation.23 | loop fusion | flops 12582912 | bytes 16777224 | tf_op jit(solution)/shard_map/convert_element_type | solution.py:57
  230.5 4.6 broadcast_select_fusion.3
  235.0 4.7 copy.104
  239.7 5.0 gather_fusion.2
  251.4 4.2 gather_fusion.3
  281.4 11.8 %all-gather.17.cloned.1.call-done = f32[2,4,1,1024,128]{4,3,2,0,1:T(8,128)} async-done(((f32[2,2,1,1024,128]{4,3,2,0,1:T(8,128)}), f32[2,4,1,1024,128]{4,3,2,0,1:T(8,128)}) %all-gather.17.cloned.1.call-update) | async-done | bytes 4194320 | tf_op jit(solution)/shard_map/all_gather | solution.py:130
  293.1 4.5 copy.165
  297.6 4.2 gather_fusion.4
  305.1 87.8 %all-reduce.3.cloned.1.call-done = f32[2,2,1024,128]{3,2,0,1:T(8,128)} async-done(((f32[2,2,1024,128]{3,2,0,1:T(8,128)}), f32[2,2,1024,128]{3,2,0,1:T(8,128)}) %all-reduce.3.cloned.1.call-update) | async-done | bytes 2097168 | tf_op jit(solution)/shard_map/psum | solution.py:134
  392.8 4.8 fusion.56
  397.9 12.5 %all-gather.15.cloned.1.call-done = f32[2,4,1024,128]{3,2,0,1:T(8,128)} async-done(((f32[2,2,1024,128]{3,2,0,1:T(8,128)}), f32[2,4,1024,128]{3,2,0,1:T(8,128)}) %all-gather.15.cloned.1.call-update) | async-done | bytes 4194320 | tf_op jit(solution)/shard_map/all_gather | solution.py:155
  410.5 4.2 gather_fusion.5
  438.4 14.9 %all-gather.19.cloned.1.call-done = f32[2,4,1,1024,128]{4,3,2,0,1:T(8,128)} async-done(((f32[2,2,1,1024,128]{4,3,2,0,1:T(8,128)}), f32[2,4,1,1024,128]{4,3,2,0,1:T(8,128)}) %all-gather.19.cloned.1.call-update) | async-done | bytes 4194320 | tf_op jit(solution)/shard_map/all_gather | solution.py:130
  453.3 4.5 copy.164
  465.4 84.6 %all-reduce.5.cloned.1.call-done = f32[2,2,1024,128]{3,2,0,1:T(8,128)} async-done(((f32[2,2,1024,128]{3,2,0,1:T(8,128)}), f32[2,2,1024,128]{3,2,0,1:T(8,128)}) %all-reduce.5.cloned.1.call-update) | async-done | bytes 2097168 | tf_op jit(solution)/shard_map/psum | solution.py:134
  (148 shorter events, 126.3 us)
Async XLA Ops:
  7.2 34.3 %all-gather.9.cloned.1.call-start = ((), (), s32[]{:S(2)}) async-start(), calls=%async_computation | async-start | bytes 2359296 | tf_op jit(solution)/shard_map/all_gather | solution.py:77
  7.9 91.4 %all-gather.11.cloned.1.call-start = ((), (), s32[]{:S(2)}) async-start(), calls=%async_computation.1 | async-start | bytes 1179648 | tf_op jit(solution)/shard_map/all_gather | solution.py:78
  9.4 23.5 %collective-permute-start.2 = (f32[1]{0:T(128)}, f32[1]{0:T(128)}, u32[]{:S(2)}, u32[]{:S(2)}) collective-permute-start(f32[1]{0:T(128)} %bitcast.16), channel_id=1, source_target_pairs={{0,8},{8,0},{16,24},{24,16},{1,9},{9,1},{17,25},{25,17},{2,10},{10... | collective-permute-start | bytes 20 | tf_op jit(solution)/shard_map/ppermute | solution.py:48
  12.4 222.6 %all-gather.13.cloned.1.call-start = ((), (), s32[]{:S(2)}) async-start(), calls=%async_computation.2 | async-start | bytes 4718592 | tf_op jit(solution)/shard_map/all_gather | solution.py:91
  30.4 11.0 %copy-start.9 = (bf16[256,2048]{0,1:T(8,128)(2,1)S(1)}, bf16[256,2048]{0,1:T(8,128)(2,1)}, u32[]{:S(2)}) copy-start(bf16[256,2048]{0,1:T(8,128)(2,1)} %bitcast_select_fusion) | copy-start | bytes 3145732
  34.3 5.2 collective-permute-start.3
  103.3 11.6 %collective-permute-start = (f32[2,256,128]{2,1,0:T(8,128)S(1)}, f32[2,256,128]{2,1,0:T(8,128)S(1)}, u32[]{:S(2)}, u32[]{:S(2)}) collective-permute-start(f32[2,256,128]{2,1,0:T(8,128)S(1)} %slice_bitcast_fusion.8), channel_id=1, source_target_pairs={{0,8},{8,0},{16,24},{24,16},{1,9},{9,1},{17,25},{25,17},{2,10},{10... | collective-permute-start | bytes 786440 | tf_op jit(solution)/shard_map/ppermute | solution.py:48
  115.0 9.4 %collective-permute-start.1 = (f32[2,256,128]{2,1,0:T(8,128)S(1)}, f32[2,256,128]{2,1,0:T(8,128)S(1)}, u32[]{:S(2)}, u32[]{:S(2)}) collective-permute-start(f32[2,256,128]{2,1,0:T(8,128)S(1)} %fusion.72), channel_id=1, source_target_pairs={{0,16},{8,24},{1,17},{9,25},{2,18},{10,26},{3,19},{11,27},{4,20},{... | collective-permute-start | bytes 786440 | tf_op jit(solution)/shard_map/ppermute | solution.py:48
  122.6 47.5 %collective-permute-start.4 = (bf16[1,1024,1024]{2,1,0:T(8,128)(2,1)}, bf16[1,1024,1024]{2,1,0:T(8,128)(2,1)}, u32[]{:S(2)}, u32[]{:S(2)}) collective-permute-start(bf16[1,1024,1024]{2,1,0:T(8,128)(2,1)} %fusion.26), channel_id=1, source_target_pairs={{0,8},{8,0},{16,24},{24,16},{1,9},{9,1},{17,25},{25,17},{2,10},{10... | collective-permute-start | bytes 6291464 | tf_op jit(solution)/shard_map/ppermute | solution.py:48
  125.4 52.6 %copy-start.10 = (f32[2]{0:T(128)S(1)}, f32[2]{0:T(128)}, u32[]{:S(2)}) copy-start(f32[2]{0:T(128)} %param.17) | copy-start | bytes 28
  125.4 52.6 %copy-start.11 = (f32[2]{0:T(128)S(1)}, f32[2]{0:T(128)}, u32[]{:S(2)}) copy-start(f32[2]{0:T(128)} %param.19) | copy-start | bytes 28
  125.4 52.6 %copy-start.12 = (f32[2]{0:T(128)S(1)}, f32[2]{0:T(128)}, u32[]{:S(2)}) copy-start(f32[2]{0:T(128)} %param.18) | copy-start | bytes 28
  125.5 167.7 %all-gather.17.cloned.1.call-start = ((), (), s32[]{:S(2)}) async-start(), calls=%async_computation.6 | async-start | bytes 6291456 | tf_op jit(solution)/shard_map/all_gather | solution.py:130
  175.1 46.2 %collective-permute-start.5 = (bf16[1,1024,1024]{2,1,0:T(8,128)(2,1)}, bf16[1,1024,1024]{2,1,0:T(8,128)(2,1)}, u32[]{:S(2)}, u32[]{:S(2)}) collective-permute-start(bf16[1,1024,1024]{2,1,0:T(8,128)(2,1)} %fusion.18), channel_id=1, source_target_pairs={{0,16},{8,24},{1,17},{9,25},{2,18},{10,26},{3,19},{11,27},{4,20},{... | collective-permute-start | bytes 6291464 | tf_op jit(solution)/shard_map/ppermute | solution.py:48
  178.0 10.2 %copy-start.13 = (s32[16]{0:T(128)S(1)}, s32[16]{0:T(128)}, u32[]{:S(2)}) copy-start(s32[16]{0:T(128)} %constant.138) | copy-start | bytes 196
  183.2 3.7 collective-permute-start.6
  186.9 34.3 %collective-permute-start.7 = (f32[1,1024]{1,0:T(1,128)S(1)}, f32[1,1024]{1,0:T(1,128)S(1)}, u32[]{:S(2)}, u32[]{:S(2)}) collective-permute-start(f32[1,1024]{1,0:T(1,128)S(1)} %fusion.71), channel_id=1, source_target_pairs={{0,16},{8,24},{1,17},{9,25},{2,18},{10,26},{3,19},{11,27},{4,20},{... | collective-permute-start | bytes 12296 | tf_op jit(solution)/shard_map/ppermute | solution.py:48
  221.3 9.2 %slice-start = ((s8[8388608]{0:T(1024)(128)(4,1)}), s8[4194304]{0:T(1024)(128)(4,1)S(1)}, s32[]{:S(2)}) async-start(s8[8388608]{0:T(1024)(128)(4,1)} %bitcast.206), calls=%async_computation.8 | async-start | bytes 8388608
  224.6 5.9 %slice-start.1 = ((s8[8388608]{0:T(1024)(128)(4,1)}), s8[4194304]{0:T(1024)(128)(4,1)S(1)}, s32[]{:S(2)}) async-start(s8[8388608]{0:T(1024)(128)(4,1)} %bitcast.206), calls=%async_computation.9 | async-start | bytes 8388608
  279.7 113.1 %all-reduce.3.cloned.1.call-start = ((), (), s32[]{:S(2)}) async-start(), calls=%async_computation.3 | async-start | bytes 4194304 | tf_op jit(solution)/shard_map/psum | solution.py:134
  305.0 105.5 %all-gather.15.cloned.1.call-start = ((), (), s32[]{:S(2)}) async-start(), calls=%async_computation.4 | async-start | bytes 6291456 | tf_op jit(solution)/shard_map/all_gather | solution.py:155
  397.7 55.6 %all-gather.19.cloned.1.call-start = ((), (), s32[]{:S(2)}) async-start(), calls=%async_computation.7 | async-start | bytes 6291456 | tf_op jit(solution)/shard_map/all_gather | solution.py:130
  438.3 111.7 %all-reduce.5.cloned.1.call-start = ((), (), s32[]{:S(2)}) async-start(), calls=%async_computation.5 | async-start | bytes 4194304 | tf_op jit(solution)/shard_map/psum | solution.py:134
  462.2 87.9 %copy-start.5 = (f32[2,2,1024,128]{3,2,0,1:T(8,128)S(1)}, f32[2,2,1024,128]{3,2,0,1:T(8,128)}, u32[]{:S(2)}) copy-start(f32[2,2,1024,128]{3,2,0,1:T(8,128)} %get-tuple-element.10) | copy-start | bytes 6291460
  (8 other events, 22.2 us)
Sparse Core Ops, SparseCore 0:
  9.6 31.7 all-gather.8
  43.0 21.6 all-gather.10
  125.5 46.7 all-gather.12
  279.8 13.2 all-gather.16
  305.1 87.6 all-reduce.2
  397.8 12.6 all-gather.14
  438.4 14.8 all-gather.18
  462.3 87.6 all-reduce.4

commit v2 on v1

--- a/solution.py
+++ b/solution.py
@@ -4,9 +4,13 @@
 import jax.numpy as jnp
 import numpy as np
 from jax import lax
+from jax.experimental import pallas as pl
+from jax.experimental.pallas import tpu as pltpu
 from jax.sharding import PartitionSpec as P
 
 ITERS = 2
+ROW_BLOCK = 256
+WIRE = jnp.float16
 SINE = (3.141582022142075, -5.16714279609351, 2.5418990253836506, -0.5546361920474749)
 
 
@@ -57,9 +61,188 @@
     return high, (x - high.astype(jnp.float32)).astype(jnp.bfloat16)
 
 
-def product(spec, a, b):
-    dot = lambda x, y: jnp.einsum(spec, x, y, preferred_element_type=jnp.float32)
-    return dot(a[0], b[0]) + dot(a[0], b[1]) + dot(a[1], b[0])
+def iterate_kernel(
+    steps, rhs, own, above_hi, above_lo, below_hi, below_lo, iterate, residual,
+    image, heading, inbox, cat, cat_t, prod, prod_t,
+    core_send, core_recv, head_send, head_recv, chain_send, chain_recv,
+):
+    chips, cores = lax.axis_size("trow"), lax.axis_size("tcol")
+    z, c = lax.axis_index("trow"), lax.axis_index("tcol")
+    other = cores - 1 - c
+    nf, share, w, tgt = iterate.shape
+    table = pair_table(chips, cores)
+    per = table.shape[3]
+    block = min(w, ROW_BLOCK)
+    mesh_id = pl.DeviceIdType.MESH
+    f32, bf16 = jnp.float32, jnp.bfloat16
+    diagonal = z == 0
+
+    def lookup(core, side, i):
+        found = jnp.int32(0)
+        for place in range(chips):
+            for one in range(cores):
+                hit = jnp.logical_and(z == place, core == one)
+                found = jnp.where(hit, jnp.int32(int(table[place, one, side, i])), found)
+        return found
+
+    mine = [lookup(c, side, i) for side in range(2) for i in range(per)]
+    theirs = [lookup(other, side, i) for side in range(2) for i in range(per)]
+
+    barrier = pltpu.get_barrier_semaphore()
+    ways = ((z > 0, z - 1), (z < chips - 1, z + 1))
+    pl.semaphore_signal(barrier, inc=1, device_id={"tcol": other}, device_id_type=mesh_id)
+    for there, place in ways:
+        @pl.when(there)
+        def _():
+            pl.semaphore_signal(barrier, inc=1, device_id={"trow": place}, device_id_type=mesh_id)
+    peers = jnp.int32(1)
+    for there, _ in ways:
+        peers = peers + jnp.where(there, jnp.int32(1), jnp.int32(0))
+    pl.semaphore_wait(barrier, peers)
+
+    def to_core(ref, slot, send, recv):
+        return pltpu.make_async_remote_copy(
+            src_ref=ref.at[slot], dst_ref=ref.at[slot], send_sem=send, recv_sem=recv,
+            device_id={"tcol": other}, device_id_type=mesh_id,
+        )
+
+    def hop(turn, way, f, j, i, source):
+        place = (z + 1) if way == 0 else (z - 1)
+        at = pl.ds(i * block, block)
+        return pltpu.make_async_remote_copy(
+            src_ref=source.at[at], dst_ref=inbox.at[turn, way, f, j, at],
+            send_sem=chain_send.at[turn, way, f, j, i], recv_sem=chain_recv.at[turn, way, f, j, i],
+            device_id={"trow": place}, device_id_type=mesh_id,
+        )
+
+    middle = chips // 2
+    end = jnp.logical_or(z == 0, z == chips - 1)
+    sides = ((z < middle, 0, z > 0, z == middle - 1), (z >= middle, 1, z < chips - 1, z == middle))
+
+    def inward(turn, f, j, i):
+        at = pl.ds(i * block, block)
+        for here, way, outer, _ in sides:
+            @pl.when(jnp.logical_and(here, outer))
+            def _():
+                hop(turn, way, f, j, i, inbox.at[turn, way, f, j]).wait_recv()
+                image[turn, f, c * share + j, at] += inbox[turn, way, f, j, at]
+
+            @pl.when(here)
+            def _():
+                hop(turn, way, f, j, i, image.at[turn, f, c * share + j]).start()
+
+    def outward(turn, f, j, i):
+        at = pl.ds(i * block, block)
+        for here, way, outer, inner in sides:
+            @pl.when(here)
+            def _():
+                hop(turn, 1 - way, f, j, i, inbox.at[turn, 1 - way, f, j]).wait_recv()
+
+            @pl.when(inner)
+            def _():
+                inbox[turn, 1 - way, f, j, at] += image[turn, f, c * share + j, at]
+
+            @pl.when(jnp.logical_and(here, outer))
+            def _():
+                hop(turn, 1 - way, f, j, i, inbox.at[turn, 1 - way, f, j]).start()
+
+    def direction(turn, f, k):
+        if turn == 0:
+            return rhs[f, k] * steps[f, 0]
+        return heading[turn - 1, f, k]
+
+    def split(x):
+        high = x.astype(bf16)
+        return high, (x - high.astype(f32)).astype(bf16)
+
+    def multiply(turn, f, m):
+        dl, dr = direction(turn, f, mine[m]), direction(turn, f, mine[per + m])
+        for k, x in enumerate((jnp.where(diagonal, dl, dr), dr)):
+            high, low = split(x)
+            cat[k, :, :tgt] = high
+            cat[k, :, tgt:] = low
+        for k, x in enumerate((dl, jnp.where(diagonal, dr, dl))):
+            high, low = split(x.T)
+            cat_t[k, :tgt, :] = high
+            cat_t[k, tgt:, :] = low
+        prod_t[...] = jnp.zeros_like(prod_t)
+
+        def rows(i, carry):
+            at = pl.ds(pl.multiple_of(i * block, block), block)
+            for k, (hi, lo) in enumerate(((above_hi, above_lo), (below_hi, below_lo))):
+                a, b = hi[f, m, at, :], lo[f, m, at, :]
+                wide = jnp.dot(a, cat[k], preferred_element_type=f32)
+                thin = jnp.dot(b, cat[k, :, :tgt], preferred_element_type=f32)
+                prod[k, at, :] = wide[:, :tgt] + wide[:, tgt:] + thin
+                d = cat_t[k, :, at]
+                wide = jnp.dot(d, a, preferred_element_type=f32)
+                thin = jnp.dot(d[:tgt], b, preferred_element_type=f32)
+                prod_t[k] += wide[:tgt] + wide[tgt:] + thin
+            return carry
+
+        lax.fori_loop(0, w // block, rows, 0)
+        three, four = prod_t[0].T, prod_t[1].T
+        two = prod[1]
+        image[turn, f, mine[m]] = prod[0] + jnp.where(diagonal, three, two)
+        image[turn, f, mine[per + m]] = four + jnp.where(diagonal, two, three) + own[f, m] * dr
+
+    iterate[...] = jnp.zeros_like(iterate)
+    for f in range(nf):
+        for j in range(share):
+            residual[f, j] = rhs[f, c * share + j]
+    for turn in range(ITERS):
+        if turn > 0:
+            for f in range(nf):
+                for j in range(share):
+                    to_core(heading, (turn - 1, f, other * share + j), head_send.at[turn, f, j], head_recv.at[turn, f, j]).wait_recv()
+        for f in range(nf):
+            for m in range(per):
+                multiply(turn, f, m)
+                for k in (m, per + m):
+                    to_core(image, (turn, f, mine[k]), core_send.at[turn, f, k], core_recv.at[turn, f, k]).start()
+        for f in range(nf):
+            for k in range(2 * per):
+                to_core(image, (turn, f, theirs[k]), core_send.at[turn, f, k], core_recv.at[turn, f, k]).wait_recv()
+        for f in range(nf):
+            for k in range(2 * per):
+                to_core(image, (turn, f, mine[k]), core_send.at[turn, f, k], core_recv.at[turn, f, k]).wait_send()
+        pieces = [(f, j, i) for f in range(nf) for j in range(share) for i in range(w // block)]
+
+        @pl.when(end)
+        def _():
+            for piece in pieces:
+                inward(turn, *piece)
+
+        for f in range(nf):
+            for j in range(share):
+                for i in range(w // block):
+                    @pl.when(jnp.logical_not(end))
+                    def _():
+                        inward(turn, f, j, i)
+
+                    outward(turn, f, j, i)
+                total = inbox[turn, jnp.where(z < middle, jnp.int32(1), jnp.int32(0)), f, j]
+                now = direction(turn, f, c * share + j)
+                iterate[f, j] = iterate[f, j] + now
+                left = residual[f, j] - (total + steps[f, 1] * now)
+                residual[f, j] = left
+                if turn + 1 < ITERS:
+                    heading[turn, f, c * share + j] = steps[f, 2 + 2 * turn] * now + steps[f, 3 + 2 * turn] * left
+                    to_core(heading, (turn, f, c * share + j), head_send.at[turn + 1, f, j], head_recv.at[turn + 1, f, j]).start()
+    for turn in range(ITERS):
+        for f in range(nf):
+            for j in range(share):
+                if turn > 0:
+                    to_core(heading, (turn - 1, f, c * share + j), head_send.at[turn, f, j], head_recv.at[turn, f, j]).wait_send()
+                for i in range(w // block):
+                    for here, way, outer, _ in sides:
+                        @pl.when(here)
+                        def _():
+                            hop(turn, way, f, j, i, image.at[turn, f, c * share + j]).wait_send()
+
+                        @pl.when(jnp.logical_and(here, outer))
+                        def _():
+                            hop(turn, 1 - way, f, j, i, inbox.at[turn, 1 - way, f, j]).wait_send()
 
 
 def on_device(samples, targets, frequencies, phases, valid_rows, ridge, low_bound, high_bound):
@@ -99,60 +282,72 @@
     diagonal = z == 0
     first = jnp.where(diagonal, left, right)
     second = jnp.where(diagonal, right, left)
-    upper = lax.broadcasted_iota(jnp.int32, (w, w), 0) <= lax.broadcasted_iota(jnp.int32, (w, w), 1)
-    same = jnp.eye(w, dtype=bool)
-    gram_one = jnp.einsum("fkma,fkmb->fmab", left, first, preferred_element_type=jnp.float32)
-    gram_two = jnp.einsum("fkma,fkmb->fmab", second, right, preferred_element_type=jnp.float32)
-    half = jnp.where(jnp.logical_and(diagonal, same), 0.5, 1.0).astype(jnp.float32)
-    tile = jnp.where(upper, gram_one, gram_two) * half
     own = jnp.where(diagonal, jnp.sum(right.astype(jnp.float32) ** 2, axis=1), 0.0)
-    tile = jnp.cumsum(tile, axis=0)
     own = jnp.cumsum(own, axis=0)
-    tile = (tile + fold_prefix(tile[-1], jnp.bfloat16)[None]) / prefix_count[:, None, None, None]
     own = (own + fold_prefix(own[-1], jnp.float32)[None]) / prefix_count[:, None, None]
-    high, low = halves(tile)
-    zero = jnp.zeros((), jnp.bfloat16)
-    above = (jnp.where(upper, high, zero), jnp.where(upper, low, zero))
-    below = (jnp.where(upper, zero, high), jnp.where(upper, zero, low))
-
-    def apply(direction):
-        mine = jnp.take(direction, ids, axis=1).reshape(nf, 2, per, w, tgt)
-        dl, dr = mine[:, 0], mine[:, 1]
-        hl, hr = halves(dl), halves(dr)
-        pick = lambda a, b: tuple(jnp.where(diagonal, i, j) for i, j in zip(a, b))
-        one = product("fmab,fmbt->fmat", above, pick(hl, hr))
-        two = product("fmab,fmbt->fmat", below, hr)
-        three = product("fmab,fmat->fmbt", above, hl)
-        four = product("fmab,fmat->fmbt", below, pick(hr, hl))
-        out_l = one + jnp.where(diagonal, three, two)
-        out_r = four + jnp.where(diagonal, two, three) + own[..., None] * dr
-        both = jnp.stack((out_l, out_r), 1).reshape(nf, 2 * per, w, tgt)
-        both = lax.all_gather(both, "tcol", axis=1, tiled=True)
-        chip_ids = jnp.asarray(table)[z].reshape(-1)
-        order = jnp.argsort(chip_ids)
-        wanted = lax.dynamic_slice_in_dim(order, c * (chips // cores), chips // cores, 0)
-        return lax.psum(jnp.take(both, wanted, axis=1), "trow")
-
-    expand = lambda x: x[:, None, None, None]
-    share = chips // cores
-    right_side_mine = lax.dynamic_slice_in_dim(right_side, c * share, share, 1)
-    center = expand((high_bound + low_bound) / 2.0 + ridge)
-    spread = expand((high_bound - low_bound) / 2.0)
-    shift = expand(ridge)
+    block = min(w, ROW_BLOCK)
+    upper = lax.broadcasted_iota(jnp.int32, (block, block), 0) <= lax.broadcasted_iota(jnp.int32, (block, block), 1)
+    half = jnp.where(jnp.logical_and(diagonal, jnp.eye(block, dtype=bool)), 0.5, 1.0).astype(jnp.float32)
+    most = 2.1 * nf * lax.axis_size("fold") * rows.shape[1]
+    fit = np.float32(2.0 ** min(0, math.floor(math.log2(60000.0 / most))))
+    parts = ([], [], [], [])
+    for start in range(0, w, block):
+        stop = start + block
+        one = jnp.einsum("fkma,fkmb->fmab", left[..., start:stop], first[..., start:], preferred_element_type=jnp.float32)
+        two = jnp.einsum("fkma,fkmb->fmab", second[..., start:stop], right[..., :stop], preferred_element_type=jnp.float32)
+        middle = jnp.where(upper, one[..., :block], two[..., start:]) * half
+        tile = jnp.concatenate((two[..., :start], middle, one[..., block:]), axis=3)
+        tile = jnp.cumsum(tile, axis=0)
+        tile = (tile + fold_prefix(tile[-1] * fit, WIRE)[None] / fit) / prefix_count[:, None, None, None]
+        above = (lax.broadcasted_iota(jnp.int32, (block, w), 0) + start) <= lax.broadcasted_iota(jnp.int32, (block, w), 1)
+        high, low = halves(tile)
+        zero = jnp.zeros((), jnp.bfloat16)
+        for k, x in enumerate((high, low)):
+            parts[k].append(jnp.where(above, x, zero))
+            parts[2 + k].append(jnp.where(above, zero, x))
+    matrices = [jnp.concatenate(x, axis=2) for x in parts]
+
+    center = (high_bound + low_bound) / 2.0 + ridge
+    spread = (high_bound - low_bound) / 2.0
     sigma = center / spread
     rho = 1.0 / sigma
-    whole = right_side / center
-    direction = right_side_mine / center
-    iterate = jnp.zeros_like(direction)
-    residual = right_side_mine
-    for iteration in range(ITERS):
-        iterate = iterate + direction
-        residual = residual - (apply(whole) + shift * direction)
-        if iteration + 1 < ITERS:
-            rho_next = 1.0 / (2.0 * sigma - rho)
-            direction = rho_next * rho * direction + 2.0 * rho_next / spread * residual
-            rho = rho_next
-            whole = lax.all_gather(direction, "tcol", axis=1, tiled=True)
+    steps = [1.0 / center, ridge]
+    for iteration in range(ITERS - 1):
+        rho_next = 1.0 / (2.0 * sigma - rho)
+        steps += [rho_next * rho, 2.0 * rho_next / spread]
+        rho = rho_next
+    steps = jnp.stack(steps, axis=1)
+    share = chips // cores
+    own = jnp.broadcast_to(own[..., None], own.shape + (tgt,))
+    block_shape = (nf, share, w, tgt)
+    vmem = pl.BlockSpec(memory_space=pltpu.VMEM)
+    f32, bf16 = jnp.float32, jnp.bfloat16
+    dma = pltpu.SemaphoreType.DMA
+    iterate, residual = pl.pallas_call(
+        iterate_kernel,
+        out_shape=[jax.ShapeDtypeStruct(block_shape, f32)] * 2,
+        in_specs=[pl.BlockSpec(memory_space=pltpu.SMEM)] + [vmem] * 6,
+        out_specs=[vmem] * 2,
+        scratch_shapes=[
+            pltpu.VMEM((ITERS, nf, chips, w, tgt), f32),
+            pltpu.VMEM((max(ITERS - 1, 1), nf, chips, w, tgt), f32),
+            pltpu.VMEM((ITERS, 2, nf, share, w, tgt), f32),
+            pltpu.VMEM((2, w, 2 * tgt), bf16),
+            pltpu.VMEM((2, 2 * tgt, w), bf16),
+            pltpu.VMEM((2, w, tgt), f32),
+            pltpu.VMEM((2, tgt, w), f32),
+            dma((ITERS, nf, 2 * per)),
+            dma((ITERS, nf, 2 * per)),
+            dma((ITERS, nf, share)),
+            dma((ITERS, nf, share)),
+            dma((ITERS, 2, nf, share, w // block)),
+            dma((ITERS, 2, nf, share, w // block)),
+        ],
+        compiler_params=pltpu.CompilerParams(
+            collective_id=0, has_side_effects=True, vmem_limit_bytes=60 * 2**20
+        ),
+        name="iterations",
+    )(steps, right_side, own, *matrices)
     shape = (nf, share * w, tgt)
     return (iterate.reshape(shape), residual.reshape(shape))
 

time: 565 us -> 469 us (0.83)
  waiting for transfers between devices: 296 us -> 53.5 us
  Pallas kernels: 0 us -> 202 us
  matrix products: 98.5 us -> 69.6 us
  local copies, waits for them, and re-layouts: 66 us -> 43.2 us
  other arithmetic: 65.6 us -> 46.8 us
  starting transfers between devices: 18.8 us -> 31 us
    pallas_call x0 -> x1, Pallas kernels: none -> 202 us  [on_device(): pl.pallas_call(iterate_kernel, out_shape=[jax.ShapeDtypeStruct(block_shap...]
    psum x2 -> x0, waiting for transfers between devices: 172 us -> none  [apply(): return lax.psum(jnp.take(both, wanted, axis=1), 'trow')]
    all_gather x3 -> x0, waiting for transfers between devices: 39.2 us -> none  [the longest x2 26.7 us: apply(): both = lax.all_gather(both, 'tcol', axis=1, tiled=True)]
    ppermute x8 -> x14, waiting for transfers between devices: 81.9 us -> 47.6 us  [fold_prefix(): got = lax.ppermute(total.astype(wire), 'fold', pairs).astype(total.dtype)]
    dot_general x26 -> x8, matrix products: 70.6 us -> 44.1 us  [the longest x4 24.7 us: on_device(): jnp.einsum('fkma,fkmb->fmab', left[..., start:stop], first[..., start:],...]
    gather x4 -> x0, local copies, waits for them, and re-layouts: 15.4 us -> none  [the longest x2 8.37 us: apply(): mine = jnp.take(direction, ids, axis=1).reshape(nf, 2, per, w, tgt)]
    ppermute x8 -> x14, starting transfers between devices: 18.2 us -> 30.9 us  [fold_prefix(): got = lax.ppermute(total.astype(wire), 'fold', pairs).astype(total.dtype)]
    all_gather x2 -> x0, local copies, waits for them, and re-layouts: 9 us -> none  [apply(): both = lax.all_gather(both, 'tcol', axis=1, tiled=True)]
  transfers between devices with their start and end apart: 16 -> 17, of which waited for: 10 -> 8; matrix products, arithmetic and copies ran while one was open for 22% -> 30% of each run, Pallas kernels for 0% -> 0%
where the time goes in v2:
time: 469 us; the launch traced here: 463 us
  Pallas kernels  202 us (43%)
  matrix products  69.6 us (15%)
  waiting for transfers between devices  53.5 us (11%)
  other arithmetic  46.8 us (10%)
  local copies, waits for them, and re-layouts  43.2 us (9%)
  starting transfers between devices  31 us (7%)
  between operations  17.3 us (4%)
    pallas_call x1, Pallas kernels, on_device(): pl.pallas_call(iterate_kernel, out_shape=[jax.ShapeDtypeStruct(block_shap...  202 us
    ppermute x14, waiting for transfers between devices, fold_prefix(): got = lax.ppermute(total.astype(wire), 'fold', pairs).astype(total.dtype)  47.6 us
    ppermute x14, starting transfers between devices, fold_prefix(): got = lax.ppermute(total.astype(wire), 'fold', pairs).astype(total.dtype)  30.9 us
    dot_general x4, matrix products, on_device(): jnp.einsum('fkma,fkmb->fmab', left[..., start:stop], first[..., start:],...  24.7 us
    dot_general x1, matrix products, features(): jnp.einsum('fkr,rc->fkc', sample_rows, freq_cols, preferred_element_type=...  21.6 us
    dot_general x4, matrix products, on_device(): jnp.einsum('fkma,fkmb->fmab', second[..., start:stop], right[..., :stop],...  19.4 us
    unnamed x47, local copies, waits for them, and re-layouts  10.2 us
  transfers between devices with their start and end apart: 17, of which 8 were waited for; matrix products, arithmetic and copies ran while one was open for 30% of the time, Pallas kernels for 0%

profile of v2, /device:TPU:0, one launch (start us, length us, event | category | flops | bytes accessed | tf_op | source)
XLA Modules:
  0.0 463.3 jit_solution(123671716793520505)
XLA Ops:
  30.2 4.8 %collective-permute-start.3 = (f32[1]{0:T(128)}, f32[1]{0:T(128)}, u32[]{:S(2)}, u32[]{:S(2)}) collective-permute-start(f32[1]{0:T(128)} %add.342), channel_id=1, source_target_pairs={{0,16},{8,24},{1,17},{9,25},{2,18},{10,26},{3,19},{11,27},{4,20},{... | collective-permute-start | bytes 20 | tf_op jit(solution)/shard_map/ppermute | solution.py:52
  36.3 5.1 %all-gather.4.cloned.1.call-done = bf16[2,2048,256]{2,1,0:T(8,128)(2,1)} async-done(((bf16[2,256,256]{2,1,0:T(8,128)(2,1)}), bf16[2,2048,256]{2,1,0:T(8,128)(2,1)}) %all-gather.4.cloned.1.call-update) | async-done | bytes 2097168 | tf_op jit(solution)/shard_map/all_gather | solution.py:260
  41.4 21.6 %select_convert_fusion = bf16[2,2048,2048]{1,2,0:T(8,128)(2,1)S(1)} fusion(f32[2048]{0:T(1024)S(1)} %fusion.75, pred[2,2048]{1,0:T(4,128)(4,1)S(1)} %iota_compare_fusion.6, bf16[2,2048,256]{2,1,0:T(8,128)(2,1)} %all-gather.4.cloned.1.call-done, bf16[256,2048]{0,1:T(8,128)(2,1)S(1)} %bitcast_select_fusion.4), kind=kOutput, calls=%fused_computation.4 | convolution fusion | flops 4437573632 | bytes 19935232 | tf_op jit(solution)/shard_map/fkr,rc->fkc/dot_general | solution.py:30
  63.0 6.7 %broadcast_select_fusion.1 = (bf16[2,2048,1,1024]{1,3,0,2:T(8,128)(2,1)}, bf16[2,2048,1,1024]{1,3,0,2:T(8,128)(2,1)}) fusion(pred[]{:T(512)S(6)} %eq.10, bf16[2,2048,2,1,1024]{1,4,2,0,3:T(8,128)(2,1)S(1)} %bitcast.253), kind=kLoop, calls=%fused_computation.14 | loop fusion | flops 8388608 | bytes 33554432 | tf_op jit(solution)/shard_map/jit(_where)/select_n | solution.py:284
  69.7 8.5 %slice_bitcast_fusion.1 = (bf16[2,2048,1,1024]{1,3,0,2:T(8,128)(2,1)}, bf16[2,2048,1,1024]{1,3,0,2:T(8,128)(2,1)}) fusion(bf16[2,2048,2,1,1024]{1,4,2,0,3:T(8,128)(2,1)S(1)} %bitcast.254), kind=kLoop, calls=%fused_computation.19 | loop fusion | bytes 33554432 | tf_op jit(solution)/shard_map/squeeze | solution.py:264
  78.3 5.8 %fusion.43 = f32[2,1,256,768]{3,2,1,0:T(8,128)S(1)} fusion(bf16[2,2048,1,1024]{1,3,0,2:T(8,128)(2,1)} %get-tuple-element.20, bf16[2,2048,1,1024]{1,3,0,2:T(8,128)(2,1)} %get-tuple-element.22), kind=kOutput, calls=%fused_computation.79 | convolution fusion | flops 1610612736 | bytes 9961472 | tf_op jit(solution)/shard_map/fkma,fkmb->fmab/dot_general | solution.py:297
  84.1 5.7 %fusion.44 = f32[2,1,256,512]{3,2,1,0:T(8,128)} fusion(bf16[2,2048,1,1024]{1,3,0,2:T(8,128)(2,1)} %get-tuple-element.20, bf16[2,2048,1,1024]{1,3,0,2:T(8,128)(2,1)} %get-tuple-element.22), kind=kOutput, calls=%fused_computation.80 | convolution fusion | flops 1073741824 | bytes 7340032 | tf_op jit(solution)/shard_map/fkma,fkmb->fmab/dot_general | solution.py:297
  89.8 5.2 %fusion.42 = f32[2,1,256,768]{3,2,1,0:T(8,128)S(1)} fusion(bf16[2,2048,1,1024]{1,3,0,2:T(8,128)(2,1)} %get-tuple-element.23, bf16[2,2048,1,1024]{1,3,0,2:T(8,128)(2,1)} %get-tuple-element.21), kind=kOutput, calls=%fused_computation.78 | convolution fusion | flops 1610612736 | bytes 9961472 | tf_op jit(solution)/shard_map/fkma,fkmb->fmab/dot_general | solution.py:296
  95.0 5.6 %fusion.45 = f32[2,1,256,512]{3,2,1,0:T(8,128)} fusion(bf16[2,2048,1,1024]{1,3,0,2:T(8,128)(2,1)} %get-tuple-element.23, bf16[2,2048,1,1024]{1,3,0,2:T(8,128)(2,1)} %get-tuple-element.21), kind=kOutput, calls=%fused_computation.81 | convolution fusion | flops 1073741824 | bytes 7340032 | tf_op jit(solution)/shard_map/fkma,fkmb->fmab/dot_general | solution.py:296
  100.7 4.1 fusion.39
  120.1 10.7 %fusion.38 = f32[2,1,256,1024]{3,2,1,0:T(8,128)} fusion(pred[]{:T(512)S(6)} %eq.10, bf16[2,2048,2,1,1024]{1,4,2,0,3:T(8,128)(2,1)} %bitcast.257, bf16[2,2048,1,1024]{1,3,0,2:T(8,128)(2,1)} %get-tuple-element.21), kind=kOutput, calls=%fused_computation.76 | convolution fusion | flops 2151677952 | bytes 20971520 | tf_op jit(solution)/shard_map/fkma,fkmb->fmab/dot_general | solution.py:296
  139.0 14.8 %collective-permute-done = f32[2,256,128]{2,1,0:T(8,128)S(1)} collective-permute-done((f32[2,256,128]{2,1,0:T(8,128)}, f32[2,256,128]{2,1,0:T(8,128)S(1)}, u32[]{:S(2)}, u32[]{:S(2)}) %collective-permute-start) | collective-permute-done | bytes 262176 | tf_op jit(solution)/shard_map/ppermute | solution.py:52
  157.3 3.9 fusion.51
  165.2 4.5 collective-permute-start.5
  172.6 3.9 collective-permute-start.9
  183.7 5.2 %collective-permute-done.9 = f16[1,256,1024]{2,1,0:T(8,128)(2,1)S(1)} collective-permute-done((f16[1,256,1024]{2,1,0:T(8,128)(2,1)S(1)}, f16[1,256,1024]{2,1,0:T(8,128)(2,1)S(1)}, u32[]{:S(2)}, u32[]{:S(2)}) %collective-permute-start.9) | collective-permute-done | bytes 524320 | tf_op jit(solution)/shard_map/ppermute | solution.py:52
  190.1 10.0 %collective-permute-done.13 = f16[1,256,1024]{2,1,0:T(8,128)(2,1)S(1)} collective-permute-done((f16[1,256,1024]{2,1,0:T(8,128)(2,1)S(1)}, f16[1,256,1024]{2,1,0:T(8,128)(2,1)S(1)}, u32[]{:S(2)}, u32[]{:S(2)}) %collective-permute-start.13) | collective-permute-done | bytes 524320 | tf_op jit(solution)/shard_map/ppermute | solution.py:52
  201.4 10.0 %collective-permute-done.11 = f16[1,256,1024]{2,1,0:T(8,128)(2,1)S(1)} collective-permute-done((f16[1,256,1024]{2,1,0:T(8,128)(2,1)S(1)}, f16[1,256,1024]{2,1,0:T(8,128)(2,1)S(1)}, u32[]{:S(2)}, u32[]{:S(2)}) %collective-permute-start.11) | collective-permute-done | bytes 524320 | tf_op jit(solution)/shard_map/ppermute | solution.py:52
  212.6 6.2 %collective-permute-done.7 = f16[1,256,1024]{2,1,0:T(8,128)(2,1)S(1)} collective-permute-done((f16[1,256,1024]{2,1,0:T(8,128)(2,1)S(1)}, f16[1,256,1024]{2,1,0:T(8,128)(2,1)S(1)}, u32[]{:S(2)}, u32[]{:S(2)}) %collective-permute-start.7) | collective-permute-done | bytes 524320 | tf_op jit(solution)/shard_map/ppermute | solution.py:52
  219.1 4.2 broadcast_select_fusion.14
  234.5 4.7 %copy.75 = f32[8,2,2,256,128]{4,3,1,2,0:T(8,128)} copy(f32[8,2,2,256,128]{4,3,2,1,0:T(8,128)} %all-gather.8.cloned.1.call-done) | data formatting | bytes 8388608 | tf_op jit(solution)/shard_map/all_gather | solution.py:274
  239.1 5.0 %gather_fusion.2 = f32[16,2,256,128]{3,2,1,0:T(8,128)} fusion(f32[16,2,256,128]{3,2,1,0:T(8,128)} %bitcast.259, s32[1024]{0:T(1024)S(1)} %pad_clamp_fusion), kind=kCustom, calls=%fused_computation.2 | custom fusion | bytes 8388672 | tf_op jit(solution)/shard_map/jit(_take)/gather | solution.py:279
  244.1 4.6 copy.76
  250.0 202.0 %iterations.1 = (f32[2,2,1024,128]{3,2,1,0:T(8,128)}, f32[2,2,1024,128]{3,2,1,0:T(8,128)}) custom-call(f32[2,4]{1,0:T(2,128)} %pad_maximum_fusion.4.steps, f32[2,4,1024,128]{3,2,1,0:T(8,128)} %bitcast.261, f32[2,1,1024,128]{3,2,1,0:T(8,128)} %broadcast_in_dim.204.own, bf16[2,1,1024,1024]{3,2,1,0:T(8,128)(2,1)} %pad_maximum_fusion.above_hi, ...), custom_call_target="tpu_custom_call" | custom-call | tf_op jit(solution)/shard_map/iterations/pallas_call | solution.py:326
  (154 shorter events, 83.2 us)
Async XLA Ops:
  7.2 34.3 %all-gather.4.cloned.1.call-start = ((), (), s32[]{:S(2)}) async-start(), calls=%async_computation | async-start | bytes 2359296 | tf_op jit(solution)/shard_map/all_gather | solution.py:260
  7.9 122.9 %all-gather.6.cloned.1.call-start = ((), (), s32[]{:S(2)}) async-start(), calls=%async_computation.1 | async-start | bytes 1179648 | tf_op jit(solution)/shard_map/all_gather | solution.py:261
  9.4 19.5 %collective-permute-start.2 = (f32[1]{0:T(128)}, f32[1]{0:T(128)}, u32[]{:S(2)}, u32[]{:S(2)}) collective-permute-start(f32[1]{0:T(128)} %bitcast.20), channel_id=1, source_target_pairs={{0,8},{8,0},{16,24},{24,16},{1,9},{9,1},{17,25},{25,17},{2,10},{10... | collective-permute-start | bytes 20 | tf_op jit(solution)/shard_map/ppermute | solution.py:52
  12.3 222.1 %all-gather.8.cloned.1.call-start = ((), (), s32[]{:S(2)}) async-start(), calls=%async_computation.2 | async-start | bytes 4718592 | tf_op jit(solution)/shard_map/all_gather | solution.py:274
  20.3 7.5 %copy-start.20 = (f32[2]{0:T(128)S(1)}, f32[2]{0:T(128)}, u32[]{:S(2)}) copy-start(f32[2]{0:T(128)} %param.15) | copy-start | bytes 28
  30.2 5.5 %collective-permute-start.3 = (f32[1]{0:T(128)}, f32[1]{0:T(128)}, u32[]{:S(2)}, u32[]{:S(2)}) collective-permute-start(f32[1]{0:T(128)} %add.342), channel_id=1, source_target_pairs={{0,16},{8,24},{1,17},{9,25},{2,18},{10,26},{3,19},{11,27},{4,20},{... | collective-permute-start | bytes 20 | tf_op jit(solution)/shard_map/ppermute | solution.py:52
  63.0 55.4 %copy-start = (bf16[2,2048,2048]{1,2,0:T(8,128)(2,1)}, bf16[2,2048,2048]{1,2,0:T(8,128)(2,1)S(1)}, u32[]{:S(2)}) copy-start(bf16[2,2048,2048]{1,2,0:T(8,128)(2,1)S(1)} %select_convert_fusion) | copy-start | bytes 50331652
  84.0 25.0 %copy-start.6 = (f32[2,1,256,768]{3,2,1,0:T(8,128)}, f32[2,1,256,768]{3,2,1,0:T(8,128)S(1)}, u32[]{:S(2)}) copy-start(f32[2,1,256,768]{3,2,1,0:T(8,128)S(1)} %fusion.43) | copy-start | bytes 4718596
  95.0 9.8 %copy-start.11 = (f32[2,1,256,768]{3,2,1,0:T(8,128)}, f32[2,1,256,768]{3,2,1,0:T(8,128)S(1)}, u32[]{:S(2)}) copy-start(f32[2,1,256,768]{3,2,1,0:T(8,128)S(1)} %fusion.42) | copy-start | bytes 4718596
  111.4 59.9 %collective-permute-start.8 = (f16[1,256,1024]{2,1,0:T(8,128)(2,1)}, f16[1,256,1024]{2,1,0:T(8,128)(2,1)}, u32[]{:S(2)}, u32[]{:S(2)}) collective-permute-start(f16[1,256,1024]{2,1,0:T(8,128)(2,1)} %fusion.67), channel_id=1, source_target_pairs={{0,8},{8,0},{16,24},{24,16},{1,9},{9,1},{17,25},{25,17},{2,10},{10... | collective-permute-start | bytes 1572872 | tf_op jit(solution)/shard_map/ppermute | solution.py:52
  114.0 62.6 %collective-permute-start.12 = (f16[1,256,1024]{2,1,0:T(8,128)(2,1)}, f16[1,256,1024]{2,1,0:T(8,128)(2,1)}, u32[]{:S(2)}, u32[]{:S(2)}) collective-permute-start(f16[1,256,1024]{2,1,0:T(8,128)(2,1)} %fusion.69), channel_id=1, source_target_pairs={{0,8},{8,0},{16,24},{24,16},{1,9},{9,1},{17,25},{25,17},{2,10},{10... | collective-permute-start | bytes 1572872 | tf_op jit(solution)/shard_map/ppermute | solution.py:52
  116.9 62.2 %collective-permute-start.10 = (f16[1,256,1024]{2,1,0:T(8,128)(2,1)}, f16[1,256,1024]{2,1,0:T(8,128)(2,1)}, u32[]{:S(2)}, u32[]{:S(2)}) collective-permute-start(f16[1,256,1024]{2,1,0:T(8,128)(2,1)} %fusion.68), channel_id=1, source_target_pairs={{0,8},{8,0},{16,24},{24,16},{1,9},{9,1},{17,25},{25,17},{2,10},{10... | collective-permute-start | bytes 1572872 | tf_op jit(solution)/shard_map/ppermute | solution.py:52
  134.9 22.4 %copy-start.14 = (f32[256,256]{1,0:T(8,128)S(1)}, f32[256,256]{1,0:T(8,128)}, u32[]{:S(2)}) copy-start(f32[256,256]{1,0:T(8,128)} %fusion.74) | copy-start | bytes 786436
  135.6 18.2 %collective-permute-start = (f32[2,256,128]{2,1,0:T(8,128)}, f32[2,256,128]{2,1,0:T(8,128)S(1)}, u32[]{:S(2)}, u32[]{:S(2)}) collective-permute-start(f32[2,256,128]{2,1,0:T(8,128)} %slice_bitcast_fusion.78), channel_id=1, source_target_pairs={{0,8},{8,0},{16,24},{24,16},{1,9},{9,1},{17,25},{25,17},{2,10},{10... | collective-permute-start | bytes 786440 | tf_op jit(solution)/shard_map/ppermute | solution.py:52
  137.5 27.7 %collective-permute-start.4 = (f32[1,1024]{1,0:T(1,128)S(1)}, f32[1,1024]{1,0:T(1,128)S(1)}, u32[]{:S(2)}, u32[]{:S(2)}) collective-permute-start(f32[1,1024]{1,0:T(1,128)S(1)} %slice_bitcast_fusion.79), channel_id=1, source_target_pairs={{0,8},{8,0},{16,24},{24,16},{1,9},{9,1},{17,25},{25,17},{2,10},{10... | collective-permute-start | bytes 12296 | tf_op jit(solution)/shard_map/ppermute | solution.py:52
  153.9 8.5 %collective-permute-start.1 = (f32[2,256,128]{2,1,0:T(8,128)S(1)}, f32[2,256,128]{2,1,0:T(8,128)S(1)}, u32[]{:S(2)}, u32[]{:S(2)}) collective-permute-start(f32[2,256,128]{2,1,0:T(8,128)S(1)} %fusion.87), channel_id=1, source_target_pairs={{0,16},{8,24},{1,17},{9,25},{2,18},{10,26},{3,19},{11,27},{4,20},{... | collective-permute-start | bytes 786440 | tf_op jit(solution)/shard_map/ppermute | solution.py:52
  163.3 13.2 %copy-start.2 = (f32[2,1,256,1024]{3,2,1,0:T(8,128)S(1)}, f32[2,1,256,1024]{3,2,1,0:T(8,128)}, u32[]{:S(2)}) copy-start(f32[2,1,256,1024]{3,2,1,0:T(8,128)} %copy-done.1) | copy-start | bytes 6291460
  163.3 15.8 %copy-start.4 = (f32[2,1,256,1024]{3,2,1,0:T(8,128)S(1)}, f32[2,1,256,1024]{3,2,1,0:T(8,128)}, u32[]{:S(2)}) copy-start(f32[2,1,256,1024]{3,2,1,0:T(8,128)} %copy-done.3) | copy-start | bytes 6291460
  165.2 6.1 %collective-permute-start.5 = (f32[1,1024]{1,0:T(1,128)S(1)}, f32[1,1024]{1,0:T(1,128)S(1)}, u32[]{:S(2)}, u32[]{:S(2)}) collective-permute-start(f32[1,1024]{1,0:T(1,128)S(1)} %fusion.86), channel_id=1, source_target_pairs={{0,16},{8,24},{1,17},{9,25},{2,18},{10,26},{3,19},{11,27},{4,20},{... | collective-permute-start | bytes 12296 | tf_op jit(solution)/shard_map/ppermute | solution.py:52
  169.8 12.1 %collective-permute-start.6 = (f16[1,256,1024]{2,1,0:T(8,128)(2,1)S(1)}, f16[1,256,1024]{2,1,0:T(8,128)(2,1)S(1)}, u32[]{:S(2)}, u32[]{:S(2)}) collective-permute-start(f16[1,256,1024]{2,1,0:T(8,128)(2,1)S(1)} %fusion.66), channel_id=1, source_target_pairs={{0,8},{8,0},{16,24},{24,16},{1,9},{9,1},{17,25},{25,17},{2,10},{10... | collective-permute-start | bytes 1572872 | tf_op jit(solution)/shard_map/ppermute | solution.py:52
  172.6 16.3 %collective-permute-start.9 = (f16[1,256,1024]{2,1,0:T(8,128)(2,1)S(1)}, f16[1,256,1024]{2,1,0:T(8,128)(2,1)S(1)}, u32[]{:S(2)}, u32[]{:S(2)}) collective-permute-start(f16[1,256,1024]{2,1,0:T(8,128)(2,1)S(1)} %fusion.57), channel_id=1, source_target_pairs={{0,16},{8,24},{1,17},{9,25},{2,18},{10,26},{3,19},{11,27},{4,20},{... | collective-permute-start | bytes 1572872 | tf_op jit(solution)/shard_map/ppermute | solution.py:52
  177.8 22.3 %collective-permute-start.13 = (f16[1,256,1024]{2,1,0:T(8,128)(2,1)S(1)}, f16[1,256,1024]{2,1,0:T(8,128)(2,1)S(1)}, u32[]{:S(2)}, u32[]{:S(2)}) collective-permute-start(f16[1,256,1024]{2,1,0:T(8,128)(2,1)S(1)} %fusion.63), channel_id=1, source_target_pairs={{0,16},{8,24},{1,17},{9,25},{2,18},{10,26},{3,19},{11,27},{4,20},{... | collective-permute-start | bytes 1572872 | tf_op jit(solution)/shard_map/ppermute | solution.py:52
  180.4 31.0 %collective-permute-start.11 = (f16[1,256,1024]{2,1,0:T(8,128)(2,1)S(1)}, f16[1,256,1024]{2,1,0:T(8,128)(2,1)S(1)}, u32[]{:S(2)}, u32[]{:S(2)}) collective-permute-start(f16[1,256,1024]{2,1,0:T(8,128)(2,1)S(1)} %fusion.60), channel_id=1, source_target_pairs={{0,16},{8,24},{1,17},{9,25},{2,18},{10,26},{3,19},{11,27},{4,20},{... | collective-permute-start | bytes 1572872 | tf_op jit(solution)/shard_map/ppermute | solution.py:52
  182.0 36.8 %collective-permute-start.7 = (f16[1,256,1024]{2,1,0:T(8,128)(2,1)S(1)}, f16[1,256,1024]{2,1,0:T(8,128)(2,1)S(1)}, u32[]{:S(2)}, u32[]{:S(2)}) collective-permute-start(f16[1,256,1024]{2,1,0:T(8,128)(2,1)S(1)} %fusion.54), channel_id=1, source_target_pairs={{0,16},{8,24},{1,17},{9,25},{2,18},{10,26},{3,19},{11,27},{4,20},{... | collective-permute-start | bytes 1572872 | tf_op jit(solution)/shard_map/ppermute | solution.py:52
  (17 other events, 67.9 us)
Sparse Core Ops, SparseCore 0:
  9.6 31.7 all-gather.3
  43.0 21.5 all-gather.5
  163.5 47.6 all-gather.7
